TPU v7x, 32 devices: a whole 2x2x4 slice. The times are simulated.
32 devices in a mesh: groups: 2 (over y), section: 4 (over z), fsdp: 4 (over x, core).
Axes of the slice: x: 2, y: 2, z: 4, core: 2. Of those that a mesh axis runs over, the one named last changes fastest.
Arguments:
- sent_act: bfloat16 [4, 1024, 4096], P('section', 'groups', 'fsdp'), parts along dimension 1, may hold values from -6 to 6
- sent_grad: bfloat16 [4, 1024, 4096], P('section', 'groups', 'fsdp'), parts along dimension 1, may hold values from -6 to 6
- stash_in: bfloat16 [4, 2, 1024, 4096], P('section', None, 'groups', 'fsdp'), parts along dimension 2, may hold values from -6 to 6
- stash_pre: bfloat16 [4, 2, 1024, 4096], P('section', None, 'groups', 'fsdp'), parts along dimension 2, may hold values from -6 to 6
- layer_weight: bfloat16 [4, 4096, 4096], P('section', None, 'fsdp'), may hold values from -0.125 to 0.125
- layer_bias: float32 [4, 4096], P('section', 'fsdp'), may hold values from -3 to 3
- seg_table: bfloat16 [4784, 4096], P('section', 'fsdp'), may hold values from -6 to 6
- seg_index: int32 [1024, 32], P('groups'), parts along dimension 0, may hold values from 0 to 4783
- seg_amp: float32 [1024, 32], P('groups'), parts along dimension 0, may hold values from -1.2 to 1.2
- field_angle: float32 [1024, 2], P('groups'), parts along dimension 0, may hold values from -1 to 1
- angle_weight: float32 [2, 4096], P(None, 'fsdp'), may hold values from -3 to 3
- target: bfloat16 [1024, 4096], P('groups', 'fsdp'), parts along dimension 0, may hold values from -6 to 6
- sched: int32 [4], P('section'), may hold values from 0 to 1
Outputs:
- fwd_out: bfloat16 [4, 1024, 4096], P('section', 'groups', 'fsdp'), parts along dimension 1
- grad_in: bfloat16 [4, 1024, 4096], P('section', 'groups', 'fsdp'), parts along dimension 1
- grad_w: bfloat16 [4, 8192, 4096], P('section', 'groups', 'fsdp'), parts along dimension 1
- grad_bias: float32 [4, 8192], P('section', ('groups', 'fsdp')), parts along dimension 1
There are 2 independent parts, one for each index of `groups`. A program takes and returns all parts, laid end to end along the dimension named above; an argument that names none is the same for every part. Nothing has to cross between parts.
All inputs are finite; a program needn't handle non-finite values.
Results may differ from a plain program's by a relative error of at most 0.017.
Values may be sent and summed in bfloat16 or wider, within the bound.
A program may use at most 128 MiB of HBM per device.

v0:
```python
import functools

import jax
import jax.numpy as jnp
from jax import lax
from jax.experimental import pallas as pl
from jax.experimental.pallas import tpu as pltpu
from jax.sharding import PartitionSpec as P

CHUNKS = 4
MESH = pl.DeviceIdType.MESH
ROOT = 0.7978845608028654
CUBIC = 0.044715


def gelu_parts(x):
    squared = x * x
    t = jnp.tanh(ROOT * (x + CUBIC * x * squared))
    half = 0.5 * (1.0 + t)
    slope = half + 0.5 * x * (1.0 - t * t) * (ROOT * (1.0 + 3.0 * CUBIC * squared))
    return x * half, slope


def gelu(x):
    return x * (0.5 * (1.0 + jnp.tanh(ROOT * (x + CUBIC * x * x * x))))


def kernel(
    sections, shards,
    act_hbm, grad_hbm, stash_ref, pre_ref, weight_hbm, bias_ref, table_ref, index_ref, amp_ref,
    field_ref, angle_ref, target_ref, sched_ref,
    fwd_ref, grad_in_ref, grad_w_hbm, grad_bias_ref,
    weight, feat, stash, from_next, matrix, emb, emb_recv, emb_send, pre_grad,
    part_send, part_recv, own, x_recv, grad_w,
    load_sem, z_send, z_recv, near_send, near_recv, far_send, far_recv, pass_send, pass_recv,
    part_send_sem, part_recv_sem, sum_send_sem, sum_recv_sem, store_sem,
):
    me = lax.axis_index("fsdp")
    sec = lax.axis_index("section")
    chips = shards // 2
    chip, core = me // 2, lax.rem(me, 2)
    partner = chip * 2 + 1 - core
    rows, width = pre_grad.shape
    part = rows // CHUNKS
    tile = min(256, width)

    def at_chip(j, c):
        return lax.rem(chip + j, chips) * 2 + c

    def span(c):
        return pl.ds(c * part, part)

    def remote(src, dst, send, recv, **where):
        return pltpu.make_async_remote_copy(
            src_ref=src, dst_ref=dst, send_sem=send, recv_sem=recv,
            device_id=where, device_id_type=MESH,
        )

    not_last = sec < sections - 1
    not_first = sec > 0

    load = pltpu.make_async_copy(weight_hbm.at[0], weight, load_sem)
    load.start()

    barrier = pltpu.get_barrier_semaphore()
    pl.semaphore_signal(barrier, inc=1, device_id={"fsdp": partner}, device_id_type=MESH)
    for j in range(1, chips):
        pl.semaphore_signal(barrier, inc=1, device_id={"fsdp": at_chip(j, core)}, device_id_type=MESH)

    @pl.when(not_last)
    def _():
        pl.semaphore_signal(barrier, inc=1, device_id={"section": sec + 1}, device_id_type=MESH)

    @pl.when(not_first)
    def _():
        pl.semaphore_signal(barrier, inc=1, device_id={"section": sec - 1}, device_id_type=MESH)

    pl.semaphore_wait(barrier, chips + jnp.where(not_last, 1, 0) + jnp.where(not_first, 1, 0))

    def act_copy(c):
        return remote(act_hbm.at[0, span(c)], feat.at[me, span(c)], z_send.at[0, c], z_recv.at[0, c], section=sec + 1)

    def grad_copy(c):
        return remote(grad_hbm.at[0, span(c)], from_next.at[span(c)], z_send.at[1, c], z_recv.at[1, c], section=sec - 1)

    def emb_copy(c):
        return remote(emb_send.at[span(c)], emb_recv.at[span(c)], z_send.at[2, c], z_recv.at[2, c], section=sec - 1)

    @pl.when(not_first)
    def _():
        for c in range(CHUNKS):
            grad_copy(c).start()

    @pl.when(not_last)
    def _():
        for c in range(CHUNKS):
            act_copy(c).start()

    def near_copy(g, buf, c, block):
        return remote(buf.at[block, span(c)], buf.at[block, span(c)], near_send.at[g, c], near_recv.at[g, c], fsdp=partner)

    def far_copy(g, buf, c, j, block):
        return remote(buf.at[block, span(c)], buf.at[block, span(c)], far_send.at[g, c, j - 1], far_recv.at[g, c, j - 1], fsdp=at_chip(j, core))

    def pass_copy(g, buf, c, j, block):
        return remote(buf.at[block, span(c)], buf.at[block, span(c)], pass_send.at[g, c, j - 1], pass_recv.at[g, c, j - 1], fsdp=partner)

    def gather_start(g, buf, c):
        for j in range(1, chips):
            far_copy(g, buf, c, j, me).start()
        near_copy(g, buf, c, me).start()

    def gather_pass(g, buf, c):
        for j in range(1, chips):
            block = at_chip(chips - j, core)
            far_copy(g, buf, c, j, block).wait_recv()
            pass_copy(g, buf, c, j, block).start()

    def gather_end(g, buf, c):
        near_copy(g, buf, c, partner).wait_recv()
        for j in range(1, chips):
            pass_copy(g, buf, c, j, at_chip(chips - j, 1 - core)).wait_recv()

    def gather_drain(g, buf, c):
        near_copy(g, buf, c, me).wait_send()
        for j in range(1, chips):
            far_copy(g, buf, c, j, me).wait_send()
            pass_copy(g, buf, c, j, at_chip(chips - j, core)).wait_send()

    slot = sched_ref[0]
    for c in range(CHUNKS):
        stash[me, span(c), :] = jnp.where(slot == 0, stash_ref[0, 0, span(c), :], stash_ref[0, 1, span(c), :])
        gather_start(0, stash, c)

    table_rows = table_ref.shape[0]
    wide = matrix.shape[1]
    base = sec * table_rows

    def amplitudes(i, carry):
        begin = pl.multiple_of(i * 16, 16)
        ids = index_ref[pl.ds(begin, 16), :]
        amps = amp_ref[pl.ds(begin, 16), :]
        position = lax.broadcasted_iota(jnp.int32, (16, wide), 1) + base
        total = jnp.zeros((16, wide), jnp.float32)
        for k in range(index_ref.shape[1]):
            total = total + jnp.where(ids[:, k : k + 1] == position, amps[:, k : k + 1], 0.0)
        matrix[pl.ds(begin, 16), :] = total.astype(jnp.bfloat16)
        return carry

    for c in range(CHUNKS):
        lax.fori_loop(c * part // 16, (c + 1) * part // 16, amplitudes, 0)
        emb[span(c), :] = jnp.dot(
            matrix[span(c), :table_rows], table_ref[...], preferred_element_type=jnp.float32
        )

        @pl.when(jnp.logical_not(not_last))
        def _():
            emb_send[span(c), :] = emb[span(c), :].astype(jnp.bfloat16)
            emb_copy(c).start()

    grad_bias_ref[...] = jnp.zeros_like(grad_bias_ref)
    for c in range(CHUNKS):
        @pl.when(not_last)
        def _():
            grad_copy(c).wait_recv()

        def backward(i, carry):
            at = pl.ds(pl.multiple_of(c * part + i * 16, 16), 16)
            saved = jnp.where(slot == 0, pre_ref[0, 0, at, :], pre_ref[0, 1, at, :]).astype(jnp.float32)
            value, slope = gelu_parts(saved)
            cotangent = jnp.where(
                not_last, from_next[at, :].astype(jnp.float32), value - target_ref[at, :].astype(jnp.float32)
            )
            result = (cotangent * slope).astype(jnp.bfloat16)
            pre_grad[at, :] = result
            grad_bias_ref[...] += jnp.sum(result.astype(jnp.float32), axis=0, keepdims=True)
            return carry

        lax.fori_loop(0, part // 16, backward, 0)

        @pl.when(not_first)
        def _():
            act_copy(c).wait_recv()
            gather_start(1, feat, c)

    load.wait()

    def input_part(j, c, into):
        block = at_chip(j, c)

        def step(t, carry):
            begin = pl.multiple_of(block * width + t * tile, tile)
            column = pl.ds(pl.multiple_of(t * tile, tile), tile)
            into[j, :, column] = lax.dot_general(
                pre_grad[...], weight[pl.ds(begin, tile), :], (((1,), (1,)), ((), ())),
                preferred_element_type=jnp.float32,
            ).astype(jnp.bfloat16)
            return carry

        lax.fori_loop(0, width // tile, step, 0)

    def part_copy(j):
        return remote(part_send.at[j], part_recv.at[j], part_send_sem.at[j], part_recv_sem.at[j], fsdp=partner)

    def sum_copy(j):
        return remote(own.at[j], x_recv.at[j - 1], sum_send_sem.at[j - 1], sum_recv_sem.at[j - 1], fsdp=at_chip(j, core))

    def chain(c):
        @pl.when(not_last)
        def _():
            emb_copy(c).wait_recv()

            def add(i, carry):
                at = pl.ds(pl.multiple_of(c * part + i * 16, 16), 16)
                total = emb[at, :] + emb_recv[at, :].astype(jnp.float32)

                @pl.when(not_first)
                def _():
                    emb_send[at, :] = total.astype(jnp.bfloat16)

                @pl.when(sec == 0)
                def _():
                    angular = (
                        field_ref[at, 0:1] * angle_ref[0:1, :] + field_ref[at, 1:2] * angle_ref[1:2, :]
                    )
                    feat[me, at, :] = (total + angular).astype(jnp.bfloat16)

                return carry

            lax.fori_loop(0, part // 16, add, 0)

            @pl.when(not_first)
            def _():
                emb_copy(c).start()

            @pl.when(sec == 0)
            def _():
                gather_start(1, feat, c)

    for j in range(1, chips):
        input_part(j, 1 - core, part_send)
        part_copy(j).start()
    for j in range(1, chips):
        input_part(j, core, own)
        part_copy(j).wait_recv()
        for c in range(CHUNKS):
            own[j, span(c), :] = (
                own[j, span(c), :].astype(jnp.float32) + part_recv[j, span(c), :].astype(jnp.float32)
            ).astype(jnp.bfloat16)
        sum_copy(j).start()
    chain(0)
    input_part(0, 1 - core, part_send)
    part_copy(0).start()
    chain(1)
    input_part(0, core, own)
    chain(2)

    def store_copy(block):
        at = pl.ds(pl.multiple_of(block * width, width), width)
        return pltpu.make_async_copy(grad_w.at[at, :], grad_w_hbm.at[0, at, :], store_sem.at[block])

    def weight_grad(block):
        def step(t, carry):
            begin = pl.multiple_of(block * width + t * tile, tile)
            column = pl.ds(pl.multiple_of(t * tile, tile), tile)
            grad_w[pl.ds(begin, tile), :] = lax.dot_general(
                stash[block, :, column], pre_grad[...], (((0,), (0,)), ((), ())),
                preferred_element_type=jnp.float32,
            ).astype(jnp.bfloat16)
            return carry

        lax.fori_loop(0, width // tile, step, 0)
        store_copy(block).start()

    for c in range(CHUNKS):
        gather_pass(0, stash, c)
    weight_grad(me)
    chain(3)
    for c in range(CHUNKS):
        gather_end(0, stash, c)
    weight_grad(partner)
    for j in range(1, chips):
        weight_grad(at_chip(j, core))
        weight_grad(at_chip(j, 1 - core))

    def forward(c):
        total = jnp.zeros((part, width), jnp.float32)
        for b in range(shards):
            total = total + jnp.dot(
                feat[b, span(c), :], weight[b * width : (b + 1) * width, :],
                preferred_element_type=jnp.float32,
            )
        fwd_ref[0, span(c), :] = gelu(total + bias_ref[...]).astype(jnp.bfloat16)

    for c in range(CHUNKS):
        gather_pass(1, feat, c)
        if c > 0:
            gather_end(1, feat, c - 1)
            forward(c - 1)
    gather_end(1, feat, CHUNKS - 1)
    forward(CHUNKS - 1)

    part_copy(0).wait_recv()
    for j in range(1, chips):
        sum_copy(j).wait_recv()
    for c in range(CHUNKS):
        total = own[0, span(c), :].astype(jnp.float32) + part_recv[0, span(c), :].astype(jnp.float32)
        for j in range(1, chips):
            total = total + x_recv[j - 1, span(c), :].astype(jnp.float32)
        grad_in_ref[0, span(c), :] = total.astype(jnp.bfloat16)

    for c in range(CHUNKS):
        gather_drain(0, stash, c)
        gather_drain(1, feat, c)
    for j in range(chips):
        part_copy(j).wait_send()
    for j in range(1, chips):
        sum_copy(j).wait_send()
    for b in range(shards):
        store_copy(b).wait()

    @pl.when(not_last)
    def _():
        for c in range(CHUNKS):
            act_copy(c).wait_send()

    @pl.when(not_first)
    def _():
        for c in range(CHUNKS):
            grad_copy(c).wait_send()
            emb_copy(c).wait_send()


def local(sections, shards, *args):
    rows, width = args[0].shape[1:]
    table_rows = args[6].shape[0]
    wide = (table_rows + 127) // 128 * 128
    chips = shards // 2
    vmem = pl.BlockSpec(memory_space=pltpu.VMEM)
    hbm = pl.BlockSpec(memory_space=pl.ANY)
    smem = pl.BlockSpec(memory_space=pltpu.SMEM)
    dma = pltpu.SemaphoreType.DMA
    half, full = jnp.bfloat16, jnp.float32
    return pl.pallas_call(
        functools.partial(kernel, sections, shards),
        out_shape=(
            jax.ShapeDtypeStruct((1, rows, width), half),
            jax.ShapeDtypeStruct((1, rows, width), half),
            jax.ShapeDtypeStruct((1, shards * width, width), half),
            jax.ShapeDtypeStruct((1, width), full),
        ),
        in_specs=[hbm, hbm, vmem, vmem, hbm] + [vmem] * 7 + [smem],
        out_specs=(vmem, vmem, hbm, vmem),
        scratch_shapes=[
            pltpu.VMEM((shards * width, width), half),
            pltpu.VMEM((shards, rows, width), half),
            pltpu.VMEM((shards, rows, width), half),
            pltpu.VMEM((rows, width), half),
            pltpu.VMEM((rows, wide), half),
            pltpu.VMEM((rows, width), full),
            pltpu.VMEM((rows, width), half),
            pltpu.VMEM((rows, width), half),
            pltpu.VMEM((rows, width), half),
            pltpu.VMEM((chips, rows, width), half),
            pltpu.VMEM((chips, rows, width), half),
            pltpu.VMEM((chips, rows, width), half),
            pltpu.VMEM((chips - 1, rows, width), half),
            pltpu.VMEM((shards * width, width), half),
            dma,
            dma((3, CHUNKS)),
            dma((3, CHUNKS)),
            dma((2, CHUNKS)),
            dma((2, CHUNKS)),
            dma((2, CHUNKS, chips - 1)),
            dma((2, CHUNKS, chips - 1)),
            dma((2, CHUNKS, chips - 1)),
            dma((2, CHUNKS, chips - 1)),
            dma((chips,)),
            dma((chips,)),
            dma((chips - 1,)),
            dma((chips - 1,)),
            dma((shards,)),
        ],
        compiler_params=pltpu.CompilerParams(
            collective_id=0, has_side_effects=True, vmem_limit_bytes=60 * 1024 * 1024
        ),
        cost_estimate=pl.CostEstimate(
            flops=6 * rows * shards * width * width, bytes_accessed=40 * rows * width, transcendentals=0
        ),
    )(*args)


def solution(mesh):
    return jax.shard_map(
        functools.partial(local, mesh.shape["section"], mesh.shape["fsdp"]),
        mesh=mesh,
        in_specs=(
            P("section", "groups", "fsdp"),
            P("section", "groups", "fsdp"),
            P("section", None, "groups", "fsdp"),
            P("section", None, "groups", "fsdp"),
            P("section", None, "fsdp"),
            P("section", "fsdp"),
            P("section", "fsdp"),
            P("groups", None),
            P("groups", None),
            P("groups", None),
            P(None, "fsdp"),
            P("groups", "fsdp"),
            P("section"),
        ),
        out_specs=(
            P("section", "groups", "fsdp"),
            P("section", "groups", "fsdp"),
            P("section", "groups", "fsdp"),
            P("section", ("groups", "fsdp")),
        ),
        check_vma=False,
    )
```

profile of v0, /device:TPU:0, one launch (start us, length us, event | category | flops | bytes accessed | tf_op | source)
XLA Modules:
  0.0 108.1 jit_solution(968931219054559292)
XLA Ops:
  1.3 1.7 %copy.17.index_ref = s32[512,32]{1,0:T(8,128)} copy(s32[512,32]{0,1:T(8,128)} %param.20) | data formatting | bytes 131072 | tf_op args[7]
  3.0 1.7 %copy.18.amp_ref = f32[512,32]{1,0:T(8,128)} copy(f32[512,32]{0,1:T(8,128)} %param.21) | data formatting | bytes 131072 | tf_op args[8]
  4.6 1.5 %copy.19.field_ref = f32[512,2]{1,0:T(8,128)} copy(f32[512,2]{0,1:T(2,128)} %param.22) | data formatting | bytes 8192 | tf_op args[9]
  6.2 89.0 %shard_map.156 = (bf16[1,512,1024]{2,1,0:T(8,128)(2,1)}, bf16[1,512,1024]{2,1,0:T(8,128)(2,1)}, bf16[1,4096,1024]{2,1,0:T(8,128)(2,1)}, f32[1,1024]{1,0:T(1,128)}) custom-call(bf16[1,512,1024]{2,1,0:T(8,128)(2,1)} %act_hbm.1, bf16[1,512,1024]{2,1,0:T(8,128)(2,1)} %grad_hbm.1, bf16[1,2,512,1024]{3,2,1,0:T(8,128)(2,1)} %stash_ref.1, ...), custom_call_target="tpu_custom_call" | custom-call | flops 12884901888 | bytes 20971520 | tf_op jit(solution)/shard_map/pallas_call | solution.py:344
  95.2 2.3 %copy.25 = bf16[1,512,1024]{2,1,0:T(8,128)(2,1)} copy(bf16[1,512,1024]{2,1,0:T(8,128)(2,1)} %get-tuple-element.8) | data formatting | bytes 2097152
  97.4 2.3 %copy.26 = bf16[1,512,1024]{2,1,0:T(8,128)(2,1)} copy(bf16[1,512,1024]{2,1,0:T(8,128)(2,1)} %get-tuple-element.9) | data formatting | bytes 2097152
  99.7 0.0 copy-start
  99.7 7.8 %copy.27 = bf16[1,4096,1024]{2,1,0:T(8,128)(2,1)} copy(bf16[1,4096,1024]{2,1,0:T(8,128)(2,1)} %get-tuple-element.10) | data formatting | bytes 16777216
  107.5 0.0 copy-done
  107.5 0.6 copy.28
Async XLA Ops:
  99.7 7.8 %copy-start = (f32[1,1024]{1,0:T(1,128)S(1)}, f32[1,1024]{1,0:T(1,128)}, u32[]{:S(2)}) copy-start(f32[1,1024]{1,0:T(1,128)} %get-tuple-element.11) | copy-start | bytes 12292
where the time goes:
time: 108 us
  Pallas kernels  89 us (82%)
  local copies, waits for them, and re-layouts  17.8 us (16%)
  between operations  1.29 us (1%)
    pallas_call x1, Pallas kernels, local(): pl.pallas_call(functools.partial(kernel, sections, shards), out_shape=(ja...  89 us
    unnamed x9, local copies, waits for them, and re-layouts  17.8 us

commit v1 on v0

v1 whole, which is shorter than its diff:
```python
import functools

import jax
import jax.numpy as jnp
from jax import lax
from jax.experimental import pallas as pl
from jax.experimental.pallas import tpu as pltpu
from jax.sharding import PartitionSpec as P

CHUNKS = 4
MESH = pl.DeviceIdType.MESH
ROOT = 0.7978845608028654
CUBIC = 0.044715


def gelu_parts(x):
    squared = x * x
    t = jnp.tanh(ROOT * (x + CUBIC * x * squared))
    half = 0.5 * (1.0 + t)
    slope = half + 0.5 * x * (1.0 - t * t) * (ROOT * (1.0 + 3.0 * CUBIC * squared))
    return x * half, slope


def gelu(x):
    return x * (0.5 * (1.0 + jnp.tanh(ROOT * (x + CUBIC * x * x * x))))


def kernel(
    sections, shards,
    act_hbm, grad_hbm, stash_hbm, pre_hbm, weight_hbm, bias_hbm, table_hbm, index_hbm, amp_hbm,
    field_hbm, angle_hbm, target_hbm, sched_ref,
    fwd_ref, grad_in_ref, grad_w_ref, grad_bias_ref,
    stash_ref, pre_ref, weight, bias_ref, table_ref, index_ref, amp_ref, field_ref, angle_ref, target_ref,
    ids, amps, fields,
    feat, stash, from_next, matrix, emb, emb_recv, emb_send, pre_grad,
    part_send, part_recv, own, x_recv,
    stash_sem, load_sem, z_send, z_recv, near_send, near_recv, far_send, far_recv, pass_send, pass_recv,
    part_send_sem, part_recv_sem, sum_send_sem, sum_recv_sem,
):
    me = lax.axis_index("fsdp")
    sec = lax.axis_index("section")
    chips = shards // 2
    chip, core = me // 2, lax.rem(me, 2)
    partner = chip * 2 + 1 - core
    rows, width = pre_grad.shape
    part = rows // CHUNKS
    tile = min(256, width)

    def at_chip(j, c):
        return lax.rem(chip + j, chips) * 2 + c

    def span(c):
        return pl.ds(c * part, part)

    def moving(c):
        return pl.ds(pl.multiple_of(c * part, part), part)

    def remote(src, dst, send, recv, **where):
        return pltpu.make_async_remote_copy(
            src_ref=src, dst_ref=dst, send_sem=send, recv_sem=recv,
            device_id=where, device_id_type=MESH,
        )

    not_last = sec < sections - 1
    not_first = sec > 0

    def stash_load(c):
        return pltpu.make_async_copy(stash_hbm.at[0, :, span(c)], stash_ref.at[:, span(c)], stash_sem.at[c])

    loads = {
        name: pltpu.make_async_copy(src, dst, load_sem.at[k])
        for k, (name, src, dst) in enumerate([
            ("index", index_hbm, index_ref),
            ("amp", amp_hbm, amp_ref),
            ("table", table_hbm, table_ref),
            ("pre", pre_hbm.at[0], pre_ref),
            ("target", target_hbm, target_ref),
            ("weight", weight_hbm.at[0], weight),
            ("bias", bias_hbm, bias_ref),
            ("field", field_hbm, field_ref),
            ("angle", angle_hbm, angle_ref),
        ])
    }
    for c in range(CHUNKS):
        stash_load(c).start()

    barrier = pltpu.get_barrier_semaphore()
    pl.semaphore_signal(barrier, inc=1, device_id={"fsdp": partner}, device_id_type=MESH)
    for j in range(1, chips):
        pl.semaphore_signal(barrier, inc=1, device_id={"fsdp": at_chip(j, core)}, device_id_type=MESH)

    @pl.when(not_last)
    def _():
        pl.semaphore_signal(barrier, inc=1, device_id={"section": sec + 1}, device_id_type=MESH)

    @pl.when(not_first)
    def _():
        pl.semaphore_signal(barrier, inc=1, device_id={"section": sec - 1}, device_id_type=MESH)

    for copy in loads.values():
        copy.start()

    pl.semaphore_wait(barrier, chips + jnp.where(not_last, 1, 0) + jnp.where(not_first, 1, 0))

    def act_copy(c):
        return remote(act_hbm.at[0, moving(c)], feat.at[me, moving(c)], z_send.at[0, c], z_recv.at[0, c], section=sec + 1)

    def grad_copy(c):
        return remote(grad_hbm.at[0, moving(c)], from_next.at[moving(c)], z_send.at[1, c], z_recv.at[1, c], section=sec - 1)

    def emb_copy(c):
        return remote(emb_send.at[moving(c)], emb_recv.at[moving(c)], z_send.at[2, c], z_recv.at[2, c], section=sec - 1)

    @pl.when(not_first)
    def _():
        for c in range(CHUNKS):
            grad_copy(c).start()

    @pl.when(not_last)
    def _():
        for c in range(CHUNKS):
            act_copy(c).start()

    def near_copy(g, buf, c, block):
        return remote(buf.at[block, moving(c)], buf.at[block, moving(c)], near_send.at[g, c], near_recv.at[g, c], fsdp=partner)

    def far_copy(g, buf, c, j, block):
        return remote(buf.at[block, moving(c)], buf.at[block, moving(c)], far_send.at[g, c, j - 1], far_recv.at[g, c, j - 1], fsdp=at_chip(j, core))

    def pass_copy(g, buf, c, j, block):
        return remote(buf.at[block, moving(c)], buf.at[block, moving(c)], pass_send.at[g, c, j - 1], pass_recv.at[g, c, j - 1], fsdp=partner)

    def gather_start(g, buf, c):
        for j in range(1, chips):
            far_copy(g, buf, c, j, me).start()
        near_copy(g, buf, c, me).start()

    def gather_pass(g, buf, c):
        for j in range(1, chips):
            block = at_chip(chips - j, core)
            far_copy(g, buf, c, j, block).wait_recv()
            pass_copy(g, buf, c, j, block).start()

    def gather_end(g, buf, c):
        near_copy(g, buf, c, partner).wait_recv()
        for j in range(1, chips):
            pass_copy(g, buf, c, j, at_chip(chips - j, 1 - core)).wait_recv()

    def gather_drain(g, buf, c):
        near_copy(g, buf, c, me).wait_send()
        for j in range(1, chips):
            far_copy(g, buf, c, j, me).wait_send()
            pass_copy(g, buf, c, j, at_chip(chips - j, core)).wait_send()

    slot = sched_ref[0]
    for c in range(CHUNKS):
        stash_load(c).wait()
        stash[me, span(c), :] = jnp.where(slot == 0, stash_ref[0, span(c), :], stash_ref[1, span(c), :])
        gather_start(0, stash, c)

    table_rows = table_ref.shape[0]
    wide = matrix.shape[1]
    base = sec * table_rows

    for name in ("index", "amp", "field", "angle", "table"):
        loads[name].wait()
    ids[...] = index_ref[...].T
    amps[...] = amp_ref[...].T
    fields[...] = jnp.concatenate([field_ref[...], jnp.zeros((6, rows), jnp.float32)], axis=0).T

    def amplitudes(i, carry):
        at = pl.ds(pl.multiple_of(i * 16, 16), 16)
        names = ids[at, :]
        weights = amps[at, :]
        position = lax.broadcasted_iota(jnp.int32, (16, wide), 1) + base
        total = jnp.zeros((16, wide), jnp.float32)
        for k in range(names.shape[1]):
            total = total + jnp.where(names[:, k : k + 1] == position, weights[:, k : k + 1], 0.0)
        matrix[at, :] = total.astype(jnp.bfloat16)
        return carry

    def embed(c, carry):
        lax.fori_loop(c * (part // 16), (c + 1) * (part // 16), amplitudes, 0)
        emb[moving(c), :] = jnp.dot(
            matrix[moving(c), :table_rows], table_ref[...], preferred_element_type=jnp.float32
        )

        @pl.when(jnp.logical_not(not_last))
        def _():
            emb_send[moving(c), :] = emb[moving(c), :].astype(jnp.bfloat16)
            emb_copy(c).start()

        return carry

    lax.fori_loop(0, CHUNKS, embed, 0)

    def input_part(j, c, into, r):
        block = at_chip(j, c)
        for t in range(width // tile):
            begin = pl.multiple_of(block * width + t * tile, tile)
            into[j, moving(r), t * tile : (t + 1) * tile] = lax.dot_general(
                pre_grad[moving(r), :], weight[pl.ds(begin, tile), :], (((1,), (1,)), ((), ())),
                preferred_element_type=jnp.float32,
            ).astype(jnp.bfloat16)

    def part_copy(j, c):
        return remote(part_send.at[j, moving(c)], part_recv.at[j, moving(c)], part_send_sem.at[j, c], part_recv_sem.at[j, c], fsdp=partner)

    def sum_copy(j, c):
        return remote(own.at[j, moving(c)], x_recv.at[j - 1, moving(c)], sum_send_sem.at[j - 1, c], sum_recv_sem.at[j - 1, c], fsdp=at_chip(j, core))

    for name in ("pre", "target", "weight", "bias"):
        loads[name].wait()
    grad_bias_ref[...] = jnp.zeros_like(grad_bias_ref)

    def backward(c, carry):
        @pl.when(not_last)
        def _():
            grad_copy(c).wait_recv()

        def step(i, carry):
            at = pl.ds(pl.multiple_of(c * part + i * 16, 16), 16)
            saved = jnp.where(slot == 0, pre_ref[0, at, :], pre_ref[1, at, :]).astype(jnp.float32)
            value, slope = gelu_parts(saved)
            cotangent = jnp.where(
                not_last, from_next[at, :].astype(jnp.float32), value - target_ref[at, :].astype(jnp.float32)
            )
            result = (cotangent * slope).astype(jnp.bfloat16)
            pre_grad[at, :] = result
            grad_bias_ref[...] += jnp.sum(result.astype(jnp.float32), axis=0, keepdims=True)
            return carry

        lax.fori_loop(0, part // 16, step, 0)

        for j in list(range(1, chips)) + [0]:
            input_part(j, 1 - core, part_send, c)
            part_copy(j, c).start()

        @pl.when(not_first)
        def _():
            act_copy(c).wait_recv()
            gather_start(1, feat, c)

        for j in list(range(1, chips)) + [0]:
            input_part(j, core, own, c)
        for j in range(1, chips):
            part_copy(j, c).wait_recv()
            own[j, moving(c), :] = (
                own[j, moving(c), :].astype(jnp.float32) + part_recv[j, moving(c), :].astype(jnp.float32)
            ).astype(jnp.bfloat16)
            sum_copy(j, c).start()
        return carry

    lax.fori_loop(0, CHUNKS, backward, 0)

    def chain(c):
        @pl.when(not_last)
        def _():
            emb_copy(c).wait_recv()

            def add(i, carry):
                at = pl.ds(pl.multiple_of(c * part + i * 16, 16), 16)
                total = emb[at, :] + emb_recv[at, :].astype(jnp.float32)

                @pl.when(not_first)
                def _():
                    emb_send[at, :] = total.astype(jnp.bfloat16)

                @pl.when(sec == 0)
                def _():
                    angular = (
                        fields[at, 0:1] * angle_ref[0:1, :] + fields[at, 1:2] * angle_ref[1:2, :]
                    )
                    feat[me, at, :] = (total + angular).astype(jnp.bfloat16)

                return carry

            lax.fori_loop(0, part // 16, add, 0)

            @pl.when(not_first)
            def _():
                emb_copy(c).start()

            @pl.when(sec == 0)
            def _():
                gather_start(1, feat, c)

    def weight_grad(block):
        def step(t, carry):
            begin = pl.multiple_of(block * width + t * tile, tile)
            column = pl.ds(pl.multiple_of(t * tile, tile), tile)
            grad_w_ref[0, pl.ds(begin, tile), :] = lax.dot_general(
                stash[block, :, column], pre_grad[...], (((0,), (0,)), ((), ())),
                preferred_element_type=jnp.float32,
            ).astype(jnp.bfloat16)
            return carry

        lax.fori_loop(0, width // tile, step, 0)

    blocks = [me, partner]
    for j in range(1, chips):
        blocks += [at_chip(j, core), at_chip(j, 1 - core)]
    weight_grad(blocks[0])
    for c in range(CHUNKS):
        gather_pass(0, stash, c)
    for c in range(CHUNKS):
        chain(c)
        if c == 0:
            for r in range(CHUNKS):
                gather_end(0, stash, r)
        for b in blocks[1 + c * (shards - 1) // CHUNKS : 1 + (c + 1) * (shards - 1) // CHUNKS]:
            weight_grad(b)

    def forward(c, carry):
        gather_pass(1, feat, c)
        for j in range(1, chips):
            sum_copy(j, c).wait_recv()
        part_copy(0, c).wait_recv()
        whole = own[0, moving(c), :].astype(jnp.float32) + part_recv[0, moving(c), :].astype(jnp.float32)
        for j in range(1, chips):
            whole = whole + x_recv[j - 1, moving(c), :].astype(jnp.float32)
        grad_in_ref[0, moving(c), :] = whole.astype(jnp.bfloat16)
        gather_end(1, feat, c)
        total = jnp.zeros((part, width), jnp.float32)
        for b in range(shards):
            total = total + jnp.dot(
                feat[b, moving(c), :], weight[b * width : (b + 1) * width, :],
                preferred_element_type=jnp.float32,
            )
        fwd_ref[0, moving(c), :] = gelu(total + bias_ref[...]).astype(jnp.bfloat16)
        return carry

    lax.fori_loop(0, CHUNKS, forward, 0)

    for c in range(CHUNKS):
        gather_drain(0, stash, c)
        gather_drain(1, feat, c)
        for j in range(chips):
            part_copy(j, c).wait_send()
        for j in range(1, chips):
            sum_copy(j, c).wait_send()

    @pl.when(not_last)
    def _():
        for c in range(CHUNKS):
            act_copy(c).wait_send()

    @pl.when(not_first)
    def _():
        for c in range(CHUNKS):
            grad_copy(c).wait_send()
            emb_copy(c).wait_send()


def store(pieces, fwd, grad_in, grad_w, grad_bias, fwd_out, grad_in_out, grad_w_out, grad_bias_out, sem):
    depth = grad_w.shape[1] // pieces
    copies = [(grad_w.at[0, pl.ds(i * depth, depth)], grad_w_out.at[0, pl.ds(i * depth, depth)]) for i in range(pieces)]
    copies += [(fwd, fwd_out), (grad_in, grad_in_out), (grad_bias, grad_bias_out)]
    copies = [pltpu.make_async_copy(src, dst, sem.at[i]) for i, (src, dst) in enumerate(copies)]
    for copy in copies:
        copy.start()
    for copy in copies:
        copy.wait()


def local(sections, shards, *args):
    args = list(args)
    rows, width = args[0].shape[1:]
    table_rows = args[6].shape[0]
    active = args[7].shape[1]
    for k in (7, 8, 9):
        args[k] = args[k].T
    wide = (table_rows + 127) // 128 * 128
    chips = shards // 2
    vmem = pl.BlockSpec(memory_space=pltpu.VMEM)
    hbm = pl.BlockSpec(memory_space=pltpu.HBM)
    smem = pl.BlockSpec(memory_space=pltpu.SMEM)
    dma = pltpu.SemaphoreType.DMA
    half, full = jnp.bfloat16, jnp.float32
    outs = (
        ((1, rows, width), half),
        ((1, rows, width), half),
        ((1, shards * width, width), half),
        ((1, width), full),
    )
    results = pl.pallas_call(
        functools.partial(kernel, sections, shards),
        out_shape=tuple(pltpu.VMEM(*out) for out in outs),
        in_specs=[hbm] * 12 + [smem],
        out_specs=(vmem,) * 4,
        scratch_shapes=[
            pltpu.VMEM((2, rows, width), half),
            pltpu.VMEM((2, rows, width), half),
            pltpu.VMEM((shards * width, width), half),
            pltpu.VMEM((1, width), full),
            pltpu.VMEM((table_rows, width), half),
            pltpu.VMEM((active, rows), jnp.int32),
            pltpu.VMEM((active, rows), full),
            pltpu.VMEM((2, rows), full),
            pltpu.VMEM((2, width), full),
            pltpu.VMEM((rows, width), half),
            pltpu.VMEM((rows, active), jnp.int32),
            pltpu.VMEM((rows, active), full),
            pltpu.VMEM((rows, 8), full),
            pltpu.VMEM((shards, rows, width), half),
            pltpu.VMEM((shards, rows, width), half),
            pltpu.VMEM((rows, width), half),
            pltpu.VMEM((rows, wide), half),
            pltpu.VMEM((rows, width), full),
            pltpu.VMEM((rows, width), half),
            pltpu.VMEM((rows, width), half),
            pltpu.VMEM((rows, width), half),
            pltpu.VMEM((chips, rows, width), half),
            pltpu.VMEM((chips, rows, width), half),
            pltpu.VMEM((chips, rows, width), half),
            pltpu.VMEM((chips - 1, rows, width), half),
            dma((CHUNKS,)),
            dma((9,)),
            dma((3, CHUNKS)),
            dma((3, CHUNKS)),
            dma((2, CHUNKS)),
            dma((2, CHUNKS)),
            dma((2, CHUNKS, chips - 1)),
            dma((2, CHUNKS, chips - 1)),
            dma((2, CHUNKS, chips - 1)),
            dma((2, CHUNKS, chips - 1)),
            dma((chips, CHUNKS)),
            dma((chips, CHUNKS)),
            dma((chips - 1, CHUNKS)),
            dma((chips - 1, CHUNKS)),
        ],
        compiler_params=pltpu.CompilerParams(
            collective_id=0, has_side_effects=True, vmem_limit_bytes=46 * 1024 * 1024
        ),
        cost_estimate=pl.CostEstimate(
            flops=6 * rows * shards * width * width, bytes_accessed=40 * rows * width, transcendentals=0
        ),
    )(*args)
    any_spec = pl.BlockSpec(memory_space=pl.ANY)
    return pl.pallas_call(
        functools.partial(store, 8),
        out_shape=tuple(jax.ShapeDtypeStruct(*out) for out in outs),
        in_specs=[any_spec] * 4,
        out_specs=(any_spec,) * 4,
        scratch_shapes=[dma((11,))],
        compiler_params=pltpu.CompilerParams(vmem_limit_bytes=1024 * 1024),
    )(*results)


def solution(mesh):
    return jax.shard_map(
        functools.partial(local, mesh.shape["section"], mesh.shape["fsdp"]),
        mesh=mesh,
        in_specs=(
            P("section", "groups", "fsdp"),
            P("section", "groups", "fsdp"),
            P("section", None, "groups", "fsdp"),
            P("section", None, "groups", "fsdp"),
            P("section", None, "fsdp"),
            P("section", "fsdp"),
            P("section", "fsdp"),
            P("groups", None),
            P("groups", None),
            P("groups", None),
            P(None, "fsdp"),
            P("groups", "fsdp"),
            P("section"),
        ),
        out_specs=(
            P("section", "groups", "fsdp"),
            P("section", "groups", "fsdp"),
            P("section", "groups", "fsdp"),
            P("section", ("groups", "fsdp")),
        ),
        check_vma=False,
    )
```

time: 108 us -> 88.8 us (0.82)
  local copies, waits for them, and re-layouts: 17.8 us -> 0 us
  Pallas kernels: 89 us -> 87.3 us
    unnamed x9 -> x0, local copies, waits for them, and re-layouts: 17.8 us -> none
    pallas_call x1 -> x2, Pallas kernels: 89 us -> 87.3 us  [the longest x1 83.3 us: local(): pl.pallas_call(functools.partial(kernel, sections, shards), out_shape=tup...]
where the time goes in v1:
time: 88.8 us; the launch traced here: 88.6 us
  Pallas kernels  87.3 us (98%)
  between operations  1.29 us (1%)
    pallas_call x1, Pallas kernels, local(): pl.pallas_call(functools.partial(kernel, sections, shards), out_shape=tup...  83.3 us
    pallas_call x1, Pallas kernels, local(): pl.pallas_call(functools.partial(store, 8), out_shape=tuple((jax.ShapeDty...  4.03 us

profile of v1, /device:TPU:0, one launch (start us, length us, event | category | flops | bytes accessed | tf_op | source)
XLA Modules:
  0.0 88.6 jit_solution(1622053102649460596)
XLA Ops:
  1.3 83.3 %shard_map.156 = (bf16[1,512,1024]{2,1,0:T(8,128)(2,1)S(1)}, bf16[1,512,1024]{2,1,0:T(8,128)(2,1)S(1)}, bf16[1,4096,1024]{2,1,0:T(8,128)(2,1)S(1)}, f32[1,1024]{1,0:T(1,128)S(1)}) custom-call(bf16[1,512,1024]{2,1,0:T(8,128)(2,1)} %act_hbm.1, bf16[1,512,1024]{2,1,0:T(8,128)(2,1)} %grad_hbm.1, bf16[1,2,512,1024]{3,2,1,0:T(8,128)(2,1)} %stash_hbm.1, ...), custom_call_target="tpu_custom_call" | custom-call | flops 12884901888 | bytes 20971520 | tf_op jit(solution)/shard_map/pallas_call | solution.py:386
  84.6 4.0 %shard_map.157 = (bf16[1,512,1024]{2,1,0:T(8,128)(2,1)}, bf16[1,512,1024]{2,1,0:T(8,128)(2,1)}, bf16[1,4096,1024]{2,1,0:T(8,128)(2,1)}, f32[1,1024]{1,0:T(1,128)}) custom-call(bf16[1,512,1024]{2,1,0:T(8,128)(2,1)S(1)} %get-tuple-element.8.fwd, bf16[1,512,1024]{2,1,0:T(8,128)(2,1)S(1)} %get-tuple-element.9.grad_in, ...), custom_call_target="tpu_custom_call" | custom-call | tf_op jit(solution)/shard_map/pallas_call | solution.py:440

commit v2 on v1

--- a/solution.py
+++ b/solution.py
@@ -113,7 +113,12 @@
 
     @pl.when(not_first)
     def _():
-        for c in range(CHUNKS):
+        for c in range(CHUNKS // 2):
+            grad_copy(c).start()
+
+    @pl.when(not_first & not_last)
+    def _():
+        for c in range(CHUNKS // 2, CHUNKS):
             grad_copy(c).start()
 
     @pl.when(not_last)
@@ -169,18 +174,18 @@
     fields[...] = jnp.concatenate([field_ref[...], jnp.zeros((6, rows), jnp.float32)], axis=0).T
 
     def amplitudes(i, carry):
-        at = pl.ds(pl.multiple_of(i * 16, 16), 16)
+        at = pl.ds(pl.multiple_of(i * 32, 32), 32)
         names = ids[at, :]
         weights = amps[at, :]
-        position = lax.broadcasted_iota(jnp.int32, (16, wide), 1) + base
-        total = jnp.zeros((16, wide), jnp.float32)
+        position = lax.broadcasted_iota(jnp.int32, (32, wide), 1) + base
+        total = jnp.zeros((32, wide), jnp.float32)
         for k in range(names.shape[1]):
             total = total + jnp.where(names[:, k : k + 1] == position, weights[:, k : k + 1], 0.0)
         matrix[at, :] = total.astype(jnp.bfloat16)
         return carry
 
     def embed(c, carry):
-        lax.fori_loop(c * (part // 16), (c + 1) * (part // 16), amplitudes, 0)
+        lax.fori_loop(c * (part // 32), (c + 1) * (part // 32), amplitudes, 0)
         emb[moving(c), :] = jnp.dot(
             matrix[moving(c), :table_rows], table_ref[...], preferred_element_type=jnp.float32
         )
@@ -194,17 +199,27 @@
 
     lax.fori_loop(0, CHUNKS, embed, 0)
 
-    def input_part(j, c, into, r):
+    @pl.when(jnp.logical_not(not_last))
+    def _():
+        for c in range(CHUNKS // 2, CHUNKS):
+            grad_copy(c).start()
+
+    deep = rows // 2
+
+    def side(h):
+        return pl.ds(h * deep, deep)
+
+    def input_part(j, c, into, h):
         block = at_chip(j, c)
         for t in range(width // tile):
             begin = pl.multiple_of(block * width + t * tile, tile)
-            into[j, moving(r), t * tile : (t + 1) * tile] = lax.dot_general(
-                pre_grad[moving(r), :], weight[pl.ds(begin, tile), :], (((1,), (1,)), ((), ())),
+            into[j, side(h), t * tile : (t + 1) * tile] = lax.dot_general(
+                pre_grad[side(h), :], weight[pl.ds(begin, tile), :], (((1,), (1,)), ((), ())),
                 preferred_element_type=jnp.float32,
             ).astype(jnp.bfloat16)
 
-    def part_copy(j, c):
-        return remote(part_send.at[j, moving(c)], part_recv.at[j, moving(c)], part_send_sem.at[j, c], part_recv_sem.at[j, c], fsdp=partner)
+    def part_copy(j, h):
+        return remote(part_send.at[j, side(h)], part_recv.at[j, side(h)], part_send_sem.at[j, h], part_recv_sem.at[j, h], fsdp=partner)
 
     def sum_copy(j, c):
         return remote(own.at[j, moving(c)], x_recv.at[j - 1, moving(c)], sum_send_sem.at[j - 1, c], sum_recv_sem.at[j - 1, c], fsdp=at_chip(j, core))
@@ -213,45 +228,62 @@
         loads[name].wait()
     grad_bias_ref[...] = jnp.zeros_like(grad_bias_ref)
 
-    def backward(c, carry):
-        @pl.when(not_last)
-        def _():
-            grad_copy(c).wait_recv()
-
-        def step(i, carry):
-            at = pl.ds(pl.multiple_of(c * part + i * 16, 16), 16)
-            saved = jnp.where(slot == 0, pre_ref[0, at, :], pre_ref[1, at, :]).astype(jnp.float32)
-            value, slope = gelu_parts(saved)
-            cotangent = jnp.where(
-                not_last, from_next[at, :].astype(jnp.float32), value - target_ref[at, :].astype(jnp.float32)
-            )
-            result = (cotangent * slope).astype(jnp.bfloat16)
-            pre_grad[at, :] = result
-            grad_bias_ref[...] += jnp.sum(result.astype(jnp.float32), axis=0, keepdims=True)
-            return carry
-
-        lax.fori_loop(0, part // 16, step, 0)
-
-        for j in list(range(1, chips)) + [0]:
-            input_part(j, 1 - core, part_send, c)
-            part_copy(j, c).start()
-
+    def feed(c):
         @pl.when(not_first)
         def _():
             act_copy(c).wait_recv()
             gather_start(1, feat, c)
 
-        for j in list(range(1, chips)) + [0]:
-            input_part(j, core, own, c)
-        for j in range(1, chips):
-            part_copy(j, c).wait_recv()
-            own[j, moving(c), :] = (
-                own[j, moving(c), :].astype(jnp.float32) + part_recv[j, moving(c), :].astype(jnp.float32)
+    def last_sums():
+        for j in range(1, chips):
+            sum_copy(j, CHUNKS - 1).start()
+
+    def backward(h):
+        first = h * CHUNKS // 2
+
+        def piece(c, carry):
+            @pl.when(not_last)
+            def _():
+                grad_copy(c).wait_recv()
+
+            def step(i, carry):
+                at = pl.ds(pl.multiple_of(c * part + i * 16, 16), 16)
+                saved = jnp.where(slot == 0, pre_ref[0, at, :], pre_ref[1, at, :]).astype(jnp.float32)
+                value, slope = gelu_parts(saved)
+                cotangent = jnp.where(
+                    not_last, from_next[at, :].astype(jnp.float32), value - target_ref[at, :].astype(jnp.float32)
+                )
+                result = (cotangent * slope).astype(jnp.bfloat16)
+                pre_grad[at, :] = result
+                grad_bias_ref[...] += jnp.sum(result.astype(jnp.float32), axis=0, keepdims=True)
+                return carry
+
+            return lax.fori_loop(0, part // 16, step, carry)
+
+        lax.fori_loop(first, first + CHUNKS // 2, piece, 0)
+        order = list(range(1, chips)) + [0]
+        for j in order:
+            input_part(j, 1 - core, part_send, h)
+            part_copy(j, h).start()
+        for j in order:
+            input_part(j, core, own, h)
+        for j in range(1, chips):
+            part_copy(j, h).wait_recv()
+            own[j, side(h), :] = (
+                own[j, side(h), :].astype(jnp.float32) + part_recv[j, side(h), :].astype(jnp.float32)
             ).astype(jnp.bfloat16)
-            sum_copy(j, c).start()
-        return carry
-
-    lax.fori_loop(0, CHUNKS, backward, 0)
+            for c in range(first, min(first + CHUNKS // 2, CHUNKS - 1)):
+                sum_copy(j, c).start()
+
+    late = sec == sections - 2
+    on_time = jnp.logical_not(late)
+    backward(0)
+    feed(0)
+    feed(1)
+
+    @pl.when(on_time)
+    def _():
+        backward(1)
 
     def chain(c):
         @pl.when(not_last)
@@ -300,26 +332,54 @@
     blocks = [me, partner]
     for j in range(1, chips):
         blocks += [at_chip(j, core), at_chip(j, 1 - core)]
-    weight_grad(blocks[0])
+    @pl.when(on_time)
+    def _():
+        weight_grad(blocks[0])
+
+    chain(0)
+    for c in range(CHUNKS // 2, CHUNKS):
+        feed(c)
     for c in range(CHUNKS):
         gather_pass(0, stash, c)
     for c in range(CHUNKS):
-        chain(c)
-        if c == 0:
-            for r in range(CHUNKS):
-                gather_end(0, stash, r)
-        for b in blocks[1 + c * (shards - 1) // CHUNKS : 1 + (c + 1) * (shards - 1) // CHUNKS]:
-            weight_grad(b)
+        gather_end(0, stash, c)
+    for c in range(1, CHUNKS + 1):
+        @pl.when(on_time)
+        def _():
+            for b in blocks[1 + (c - 1) * (shards - 1) // CHUNKS : 1 + c * (shards - 1) // CHUNKS]:
+                weight_grad(b)
+
+        if c < CHUNKS:
+            chain(c)
+            if c == CHUNKS - 1:
+                pl.when(on_time)(last_sums)
+
+    @pl.when(late)
+    def _():
+        backward(1)
+        last_sums()
+
+        def every(block, carry):
+            weight_grad(block)
+            return carry
+
+        lax.fori_loop(0, shards, every, 0)
+
+    def total_grad(c):
+        for j in range(1, chips):
+            sum_copy(j, c).wait_recv()
+        whole = own[0, moving(c), :].astype(jnp.float32) + part_recv[0, moving(c), :].astype(jnp.float32)
+        for j in range(1, chips):
+            whole = whole + x_recv[j - 1, moving(c), :].astype(jnp.float32)
+        grad_in_ref[0, moving(c), :] = whole.astype(jnp.bfloat16)
 
     def forward(c, carry):
         gather_pass(1, feat, c)
-        for j in range(1, chips):
-            sum_copy(j, c).wait_recv()
-        part_copy(0, c).wait_recv()
-        whole = own[0, moving(c), :].astype(jnp.float32) + part_recv[0, moving(c), :].astype(jnp.float32)
-        for j in range(1, chips):
-            whole = whole + x_recv[j - 1, moving(c), :].astype(jnp.float32)
-        grad_in_ref[0, moving(c), :] = whole.astype(jnp.bfloat16)
+
+        @pl.when(c > 0)
+        def _():
+            total_grad(c - 1)
+
         gather_end(1, feat, c)
         total = jnp.zeros((part, width), jnp.float32)
         for b in range(shards):
@@ -330,15 +390,19 @@
         fwd_ref[0, moving(c), :] = gelu(total + bias_ref[...]).astype(jnp.bfloat16)
         return carry
 
+    for h in range(2):
+        part_copy(0, h).wait_recv()
     lax.fori_loop(0, CHUNKS, forward, 0)
+    total_grad(CHUNKS - 1)
 
     for c in range(CHUNKS):
         gather_drain(0, stash, c)
         gather_drain(1, feat, c)
+        for j in range(1, chips):
+            sum_copy(j, c).wait_send()
+    for h in range(2):
         for j in range(chips):
-            part_copy(j, c).wait_send()
-        for j in range(1, chips):
-            sum_copy(j, c).wait_send()
+            part_copy(j, h).wait_send()
 
     @pl.when(not_last)
     def _():
@@ -424,8 +488,8 @@
             dma((2, CHUNKS, chips - 1)),
             dma((2, CHUNKS, chips - 1)),
             dma((2, CHUNKS, chips - 1)),
-            dma((chips, CHUNKS)),
-            dma((chips, CHUNKS)),
+            dma((chips, 2)),
+            dma((chips, 2)),
             dma((chips - 1, CHUNKS)),
             dma((chips - 1, CHUNKS)),
         ],

time: 88.8 us -> 79.4 us (0.89)
  Pallas kernels: 87.3 us -> 78 us
    pallas_call x1, Pallas kernels: 83.3 us -> 74 us  [local(): pl.pallas_call(functools.partial(kernel, sections, shards), out_shape=tup...]
where the time goes in v2:
time: 79.4 us; the launch traced here: 79.3 us
  Pallas kernels  78 us (98%)
  between operations  1.29 us (2%)
    pallas_call x1, Pallas kernels, local(): pl.pallas_call(functools.partial(kernel, sections, shards), out_shape=tup...  74 us
    pallas_call x1, Pallas kernels, local(): pl.pallas_call(functools.partial(store, 8), out_shape=tuple((jax.ShapeDty...  4.03 us

profile of v2, /device:TPU:0, one launch (start us, length us, event | category | flops | bytes accessed | tf_op | source)
XLA Modules:
  0.0 79.3 jit_solution(8603870815782614846)
XLA Ops:
  1.3 74.0 %shard_map.156 = (bf16[1,512,1024]{2,1,0:T(8,128)(2,1)S(1)}, bf16[1,512,1024]{2,1,0:T(8,128)(2,1)S(1)}, bf16[1,4096,1024]{2,1,0:T(8,128)(2,1)S(1)}, f32[1,1024]{1,0:T(1,128)S(1)}) custom-call(bf16[1,512,1024]{2,1,0:T(8,128)(2,1)} %act_hbm.1, bf16[1,512,1024]{2,1,0:T(8,128)(2,1)} %grad_hbm.1, bf16[1,2,512,1024]{3,2,1,0:T(8,128)(2,1)} %stash_hbm.1, ...), custom_call_target="tpu_custom_call" | custom-call | flops 12884901888 | bytes 20971520 | tf_op jit(solution)/shard_map/pallas_call | solution.py:450
  75.2 4.0 %shard_map.157 = (bf16[1,512,1024]{2,1,0:T(8,128)(2,1)}, bf16[1,512,1024]{2,1,0:T(8,128)(2,1)}, bf16[1,4096,1024]{2,1,0:T(8,128)(2,1)}, f32[1,1024]{1,0:T(1,128)}) custom-call(bf16[1,512,1024]{2,1,0:T(8,128)(2,1)S(1)} %get-tuple-element.8.fwd, bf16[1,512,1024]{2,1,0:T(8,128)(2,1)S(1)} %get-tuple-element.9.grad_in, ...), custom_call_target="tpu_custom_call" | custom-call | tf_op jit(solution)/shard_map/pallas_call | solution.py:504

commit v3 on v2

--- a/solution.py
+++ b/solution.py
@@ -64,8 +64,15 @@
     not_last = sec < sections - 1
     not_first = sec > 0
 
+    pieces = (range(2), range(CHUNKS))
+
+    def piece(g, c):
+        if g == 0:
+            return pl.ds(0, part) if c == 0 else pl.ds(part, rows - part)
+        return moving(c)
+
     def stash_load(c):
-        return pltpu.make_async_copy(stash_hbm.at[0, :, span(c)], stash_ref.at[:, span(c)], stash_sem.at[c])
+        return pltpu.make_async_copy(stash_hbm.at[0, :, piece(0, c)], stash_ref.at[:, piece(0, c)], stash_sem.at[c])
 
     loads = {
         name: pltpu.make_async_copy(src, dst, load_sem.at[k])
@@ -81,9 +88,7 @@
             ("angle", angle_hbm, angle_ref),
         ])
     }
-    for c in range(CHUNKS):
-        stash_load(c).start()
-
+    stash_load(0).start()
     barrier = pltpu.get_barrier_semaphore()
     pl.semaphore_signal(barrier, inc=1, device_id={"fsdp": partner}, device_id_type=MESH)
     for j in range(1, chips):
@@ -97,11 +102,10 @@
     def _():
         pl.semaphore_signal(barrier, inc=1, device_id={"section": sec - 1}, device_id_type=MESH)
 
+    stash_load(1).start()
     for copy in loads.values():
         copy.start()
 
-    pl.semaphore_wait(barrier, chips + jnp.where(not_last, 1, 0) + jnp.where(not_first, 1, 0))
-
     def act_copy(c):
         return remote(act_hbm.at[0, moving(c)], feat.at[me, moving(c)], z_send.at[0, c], z_recv.at[0, c], section=sec + 1)
 
@@ -111,29 +115,14 @@
     def emb_copy(c):
         return remote(emb_send.at[moving(c)], emb_recv.at[moving(c)], z_send.at[2, c], z_recv.at[2, c], section=sec - 1)
 
-    @pl.when(not_first)
-    def _():
-        for c in range(CHUNKS // 2):
-            grad_copy(c).start()
-
-    @pl.when(not_first & not_last)
-    def _():
-        for c in range(CHUNKS // 2, CHUNKS):
-            grad_copy(c).start()
-
-    @pl.when(not_last)
-    def _():
-        for c in range(CHUNKS):
-            act_copy(c).start()
-
     def near_copy(g, buf, c, block):
-        return remote(buf.at[block, moving(c)], buf.at[block, moving(c)], near_send.at[g, c], near_recv.at[g, c], fsdp=partner)
+        return remote(buf.at[block, piece(g, c)], buf.at[block, piece(g, c)], near_send.at[g, c], near_recv.at[g, c], fsdp=partner)
 
     def far_copy(g, buf, c, j, block):
-        return remote(buf.at[block, moving(c)], buf.at[block, moving(c)], far_send.at[g, c, j - 1], far_recv.at[g, c, j - 1], fsdp=at_chip(j, core))
+        return remote(buf.at[block, piece(g, c)], buf.at[block, piece(g, c)], far_send.at[g, c, j - 1], far_recv.at[g, c, j - 1], fsdp=at_chip(j, core))
 
     def pass_copy(g, buf, c, j, block):
-        return remote(buf.at[block, moving(c)], buf.at[block, moving(c)], pass_send.at[g, c, j - 1], pass_recv.at[g, c, j - 1], fsdp=partner)
+        return remote(buf.at[block, piece(g, c)], buf.at[block, piece(g, c)], pass_send.at[g, c, j - 1], pass_recv.at[g, c, j - 1], fsdp=partner)
 
     def gather_start(g, buf, c):
         for j in range(1, chips):
@@ -157,11 +146,38 @@
             far_copy(g, buf, c, j, me).wait_send()
             pass_copy(g, buf, c, j, at_chip(chips - j, core)).wait_send()
 
+
     slot = sched_ref[0]
-    for c in range(CHUNKS):
+
+    def pick(c):
+        at = piece(0, c)
         stash_load(c).wait()
-        stash[me, span(c), :] = jnp.where(slot == 0, stash_ref[0, span(c), :], stash_ref[1, span(c), :])
-        gather_start(0, stash, c)
+        stash[me, at, :] = jnp.where(slot == 0, stash_ref[0, at, :], stash_ref[1, at, :])
+
+    pick(0)
+    pl.semaphore_wait(barrier, chips + jnp.where(not_last, 1, 0) + jnp.where(not_first, 1, 0))
+    gather_start(0, stash, 0)
+
+    @pl.when(not_first)
+    def _():
+        for c in range(CHUNKS // 2):
+            grad_copy(c).start()
+
+    @pl.when(not_first & not_last)
+    def _():
+        grad_copy(CHUNKS // 2).start()
+
+    @pl.when(not_first & (sec < sections - 2))
+    def _():
+        grad_copy(CHUNKS - 1).start()
+
+    @pl.when(not_last)
+    def _():
+        for c in range(CHUNKS):
+            act_copy(c).start()
+
+    pick(1)
+    gather_start(0, stash, 1)
 
     table_rows = table_ref.shape[0]
     wide = matrix.shape[1]
@@ -221,8 +237,11 @@
     def part_copy(j, h):
         return remote(part_send.at[j, side(h)], part_recv.at[j, side(h)], part_send_sem.at[j, h], part_recv_sem.at[j, h], fsdp=partner)
 
+    def sum_rows(c):
+        return pl.ds(*((0, deep), (deep, part), (deep + part, part))[c])
+
     def sum_copy(j, c):
-        return remote(own.at[j, moving(c)], x_recv.at[j - 1, moving(c)], sum_send_sem.at[j - 1, c], sum_recv_sem.at[j - 1, c], fsdp=at_chip(j, core))
+        return remote(own.at[j, sum_rows(c)], x_recv.at[j - 1, sum_rows(c)], sum_send_sem.at[j - 1, c], sum_recv_sem.at[j - 1, c], fsdp=at_chip(j, core))
 
     for name in ("pre", "target", "weight", "bias"):
         loads[name].wait()
@@ -234,14 +253,14 @@
             act_copy(c).wait_recv()
             gather_start(1, feat, c)
 
-    def last_sums():
-        for j in range(1, chips):
-            sum_copy(j, CHUNKS - 1).start()
+    def send_sums(c):
+        for j in range(1, chips):
+            sum_copy(j, c).start()
 
     def backward(h):
         first = h * CHUNKS // 2
 
-        def piece(c, carry):
+        def unit(c, carry):
             @pl.when(not_last)
             def _():
                 grad_copy(c).wait_recv()
@@ -260,7 +279,7 @@
 
             return lax.fori_loop(0, part // 16, step, carry)
 
-        lax.fori_loop(first, first + CHUNKS // 2, piece, 0)
+        lax.fori_loop(first, first + CHUNKS // 2, unit, 0)
         order = list(range(1, chips)) + [0]
         for j in order:
             input_part(j, 1 - core, part_send, h)
@@ -272,18 +291,13 @@
             own[j, side(h), :] = (
                 own[j, side(h), :].astype(jnp.float32) + part_recv[j, side(h), :].astype(jnp.float32)
             ).astype(jnp.bfloat16)
-            for c in range(first, min(first + CHUNKS // 2, CHUNKS - 1)):
-                sum_copy(j, c).start()
-
-    late = sec == sections - 2
+            sum_copy(j, h).start()
+
+    late = (sec == sections - 2) | (sec == sections - 3)
     on_time = jnp.logical_not(late)
     backward(0)
     feed(0)
     feed(1)
-
-    @pl.when(on_time)
-    def _():
-        backward(1)
 
     def chain(c):
         @pl.when(not_last)
@@ -332,53 +346,42 @@
     blocks = [me, partner]
     for j in range(1, chips):
         blocks += [at_chip(j, core), at_chip(j, 1 - core)]
+    def rest():
+        for c in range(CHUNKS // 2, CHUNKS):
+            feed(c)
+        for c in pieces[0]:
+            gather_pass(0, stash, c)
+
     @pl.when(on_time)
     def _():
+        backward(1)
+        rest()
         weight_grad(blocks[0])
 
     chain(0)
-    for c in range(CHUNKS // 2, CHUNKS):
-        feed(c)
-    for c in range(CHUNKS):
-        gather_pass(0, stash, c)
-    for c in range(CHUNKS):
+    pl.when(late)(rest)
+    for c in pieces[0]:
         gather_end(0, stash, c)
-    for c in range(1, CHUNKS + 1):
+    for c in range(1, CHUNKS):
         @pl.when(on_time)
         def _():
-            for b in blocks[1 + (c - 1) * (shards - 1) // CHUNKS : 1 + c * (shards - 1) // CHUNKS]:
+            for b in blocks[1 + (c - 1) * (shards - 1) // (CHUNKS - 1) : 1 + c * (shards - 1) // (CHUNKS - 1)]:
                 weight_grad(b)
 
-        if c < CHUNKS:
-            chain(c)
-            if c == CHUNKS - 1:
-                pl.when(on_time)(last_sums)
-
-    @pl.when(late)
-    def _():
-        backward(1)
-        last_sums()
-
-        def every(block, carry):
-            weight_grad(block)
-            return carry
-
-        lax.fori_loop(0, shards, every, 0)
-
-    def total_grad(c):
-        for j in range(1, chips):
-            sum_copy(j, c).wait_recv()
-        whole = own[0, moving(c), :].astype(jnp.float32) + part_recv[0, moving(c), :].astype(jnp.float32)
-        for j in range(1, chips):
-            whole = whole + x_recv[j - 1, moving(c), :].astype(jnp.float32)
-        grad_in_ref[0, moving(c), :] = whole.astype(jnp.bfloat16)
-
-    def forward(c, carry):
-        gather_pass(1, feat, c)
-
-        @pl.when(c > 0)
+        chain(c)
+
+    @pl.when(sec == sections - 2)
+    def _():
+        grad_copy(CHUNKS - 1).start()
+
+    @pl.when(on_time)
+    def _():
+        send_sums(2)
+
+    def forward(stop, c, carry):
+        @pl.when(c + 1 < stop)
         def _():
-            total_grad(c - 1)
+            gather_pass(1, feat, c + 1)
 
         gather_end(1, feat, c)
         total = jnp.zeros((part, width), jnp.float32)
@@ -390,14 +393,42 @@
         fwd_ref[0, moving(c), :] = gelu(total + bias_ref[...]).astype(jnp.bfloat16)
         return carry
 
+    early = CHUNKS // 2
+
+    @pl.when(late)
+    def _():
+        gather_pass(1, feat, 0)
+        lax.fori_loop(0, early, functools.partial(forward, early), 0)
+        backward(1)
+        send_sums(2)
+
+        def every(block, carry):
+            weight_grad(block)
+            return carry
+
+        lax.fori_loop(0, shards, every, 0)
+
+    def total_grad(c):
+        at = sum_rows(c)
+        for j in range(1, chips):
+            sum_copy(j, c).wait_recv()
+        whole = own[0, at, :].astype(jnp.float32) + part_recv[0, at, :].astype(jnp.float32)
+        for j in range(1, chips):
+            whole = whole + x_recv[j - 1, at, :].astype(jnp.float32)
+        grad_in_ref[0, at, :] = whole.astype(jnp.bfloat16)
+
     for h in range(2):
         part_copy(0, h).wait_recv()
-    lax.fori_loop(0, CHUNKS, forward, 0)
-    total_grad(CHUNKS - 1)
-
-    for c in range(CHUNKS):
-        gather_drain(0, stash, c)
-        gather_drain(1, feat, c)
+    begin = jnp.where(late, early, 0)
+    gather_pass(1, feat, begin)
+    lax.fori_loop(begin, CHUNKS, functools.partial(forward, CHUNKS), 0)
+    for c in range(3):
+        total_grad(c)
+
+    for g, buf in enumerate((stash, feat)):
+        for c in pieces[g]:
+            gather_drain(g, buf, c)
+    for c in range(3):
         for j in range(1, chips):
             sum_copy(j, c).wait_send()
     for h in range(2):
@@ -438,7 +469,6 @@
     chips = shards // 2
     vmem = pl.BlockSpec(memory_space=pltpu.VMEM)
     hbm = pl.BlockSpec(memory_space=pltpu.HBM)
-    smem = pl.BlockSpec(memory_space=pltpu.SMEM)
     dma = pltpu.SemaphoreType.DMA
     half, full = jnp.bfloat16, jnp.float32
     outs = (
@@ -450,7 +480,7 @@
     results = pl.pallas_call(
         functools.partial(kernel, sections, shards),
         out_shape=tuple(pltpu.VMEM(*out) for out in outs),
-        in_specs=[hbm] * 12 + [smem],
+        in_specs=[hbm] * 12 + [pl.BlockSpec(memory_space=pltpu.SMEM)],
         out_specs=(vmem,) * 4,
         scratch_shapes=[
             pltpu.VMEM((2, rows, width), half),
@@ -478,7 +508,7 @@
             pltpu.VMEM((chips, rows, width), half),
             pltpu.VMEM((chips, rows, width), half),
             pltpu.VMEM((chips - 1, rows, width), half),
-            dma((CHUNKS,)),
+            dma((2,)),
             dma((9,)),
             dma((3, CHUNKS)),
             dma((3, CHUNKS)),
@@ -490,8 +520,8 @@
             dma((2, CHUNKS, chips - 1)),
             dma((chips, 2)),
             dma((chips, 2)),
-            dma((chips - 1, CHUNKS)),
-            dma((chips - 1, CHUNKS)),
+            dma((chips - 1, 3)),
+            dma((chips - 1, 3)),
         ],
         compiler_params=pltpu.CompilerParams(
             collective_id=0, has_side_effects=True, vmem_limit_bytes=46 * 1024 * 1024

time: 79.4 us -> 78.9 us (level)
  no operation moved by 1% of the time
where the time goes in v3:
time: 78.9 us; the launch traced here: 78.7 us
  Pallas kernels  77.4 us (98%)
  between operations  1.29 us (2%)
    pallas_call x1, Pallas kernels, local(): pl.pallas_call(functools.partial(kernel, sections, shards), out_shape=tup...  73.4 us
    pallas_call x1, Pallas kernels, local(): pl.pallas_call(functools.partial(store, 8), out_shape=tuple((jax.ShapeDty...  4.03 us

profile of v3, /device:TPU:0, one launch (start us, length us, event | category | flops | bytes accessed | tf_op | source)
XLA Modules:
  0.0 78.7 jit_solution(9045395501207915389)
XLA Ops:
  1.3 73.4 %shard_map.156 = (bf16[1,512,1024]{2,1,0:T(8,128)(2,1)S(1)}, bf16[1,512,1024]{2,1,0:T(8,128)(2,1)S(1)}, bf16[1,4096,1024]{2,1,0:T(8,128)(2,1)S(1)}, f32[1,1024]{1,0:T(1,128)S(1)}) custom-call(bf16[1,512,1024]{2,1,0:T(8,128)(2,1)} %act_hbm.1, bf16[1,512,1024]{2,1,0:T(8,128)(2,1)} %grad_hbm.1, bf16[1,2,512,1024]{3,2,1,0:T(8,128)(2,1)} %stash_hbm.1, ...), custom_call_target="tpu_custom_call" | custom-call | flops 12884901888 | bytes 20971520 | tf_op jit(solution)/shard_map/pallas_call | solution.py:480
  74.7 4.0 %shard_map.157 = (bf16[1,512,1024]{2,1,0:T(8,128)(2,1)}, bf16[1,512,1024]{2,1,0:T(8,128)(2,1)}, bf16[1,4096,1024]{2,1,0:T(8,128)(2,1)}, f32[1,1024]{1,0:T(1,128)}) custom-call(bf16[1,512,1024]{2,1,0:T(8,128)(2,1)S(1)} %get-tuple-element.8.fwd, bf16[1,512,1024]{2,1,0:T(8,128)(2,1)S(1)} %get-tuple-element.9.grad_in, ...), custom_call_target="tpu_custom_call" | custom-call | tf_op jit(solution)/shard_map/pallas_call | solution.py:534

commit v4 on v3

--- a/solution.py
+++ b/solution.py
@@ -8,6 +8,7 @@
 from jax.sharding import PartitionSpec as P
 
 CHUNKS = 4
+LAST = 32
 MESH = pl.DeviceIdType.MESH
 ROOT = 0.7978845608028654
 CUBIC = 0.044715
@@ -238,7 +239,7 @@
         return remote(part_send.at[j, side(h)], part_recv.at[j, side(h)], part_send_sem.at[j, h], part_recv_sem.at[j, h], fsdp=partner)
 
     def sum_rows(c):
-        return pl.ds(*((0, deep), (deep, part), (deep + part, part))[c])
+        return pl.ds(*((0, deep), (deep, part), (deep + part, part - LAST), (rows - LAST, LAST))[c])
 
     def sum_copy(j, c):
         return remote(own.at[j, sum_rows(c)], x_recv.at[j - 1, sum_rows(c)], sum_send_sem.at[j - 1, c], sum_recv_sem.at[j - 1, c], fsdp=at_chip(j, core))
@@ -377,6 +378,7 @@
     @pl.when(on_time)
     def _():
         send_sums(2)
+        send_sums(3)
 
     def forward(stop, c, carry):
         @pl.when(c + 1 < stop)
@@ -401,6 +403,7 @@
         lax.fori_loop(0, early, functools.partial(forward, early), 0)
         backward(1)
         send_sums(2)
+        send_sums(3)
 
         def every(block, carry):
             weight_grad(block)
@@ -428,9 +431,6 @@
     for g, buf in enumerate((stash, feat)):
         for c in pieces[g]:
             gather_drain(g, buf, c)
-    for c in range(3):
-        for j in range(1, chips):
-            sum_copy(j, c).wait_send()
     for h in range(2):
         for j in range(chips):
             part_copy(j, h).wait_send()
@@ -445,6 +445,11 @@
         for c in range(CHUNKS):
             grad_copy(c).wait_send()
             emb_copy(c).wait_send()
+
+    total_grad(3)
+    for c in range(4):
+        for j in range(1, chips):
+            sum_copy(j, c).wait_send()
 
 
 def store(pieces, fwd, grad_in, grad_w, grad_bias, fwd_out, grad_in_out, grad_w_out, grad_bias_out, sem):
@@ -520,8 +525,8 @@
             dma((2, CHUNKS, chips - 1)),
             dma((chips, 2)),
             dma((chips, 2)),
-            dma((chips - 1, 3)),
-            dma((chips - 1, 3)),
+            dma((chips - 1, 4)),
+            dma((chips - 1, 4)),
         ],
         compiler_params=pltpu.CompilerParams(
             collective_id=0, has_side_effects=True, vmem_limit_bytes=46 * 1024 * 1024

time: 78.9 us -> 78.8 us (level)
  no operation moved by 1% of the time
where the time goes in v4:
time: 78.8 us; the launch traced here: 78.6 us
  Pallas kernels  77.3 us (98%)
  between operations  1.29 us (2%)
    pallas_call x1, Pallas kernels, local(): pl.pallas_call(functools.partial(kernel, sections, shards), out_shape=tup...  73.3 us
    pallas_call x1, Pallas kernels, local(): pl.pallas_call(functools.partial(store, 8), out_shape=tuple((jax.ShapeDty...  4.03 us

profile of v4, /device:TPU:0, one launch (start us, length us, event | category | flops | bytes accessed | tf_op | source)
XLA Modules:
  0.0 78.6 jit_solution(16405136346148430283)
XLA Ops:
  1.3 73.3 %shard_map.156 = (bf16[1,512,1024]{2,1,0:T(8,128)(2,1)S(1)}, bf16[1,512,1024]{2,1,0:T(8,128)(2,1)S(1)}, bf16[1,4096,1024]{2,1,0:T(8,128)(2,1)S(1)}, f32[1,1024]{1,0:T(1,128)S(1)}) custom-call(bf16[1,512,1024]{2,1,0:T(8,128)(2,1)} %act_hbm.1, bf16[1,512,1024]{2,1,0:T(8,128)(2,1)} %grad_hbm.1, bf16[1,2,512,1024]{3,2,1,0:T(8,128)(2,1)} %stash_hbm.1, ...), custom_call_target="tpu_custom_call" | custom-call | flops 12884901888 | bytes 20971520 | tf_op jit(solution)/shard_map/pallas_call | solution.py:485
  74.6 4.0 %shard_map.157 = (bf16[1,512,1024]{2,1,0:T(8,128)(2,1)}, bf16[1,512,1024]{2,1,0:T(8,128)(2,1)}, bf16[1,4096,1024]{2,1,0:T(8,128)(2,1)}, f32[1,1024]{1,0:T(1,128)}) custom-call(bf16[1,512,1024]{2,1,0:T(8,128)(2,1)S(1)} %get-tuple-element.8.fwd, bf16[1,512,1024]{2,1,0:T(8,128)(2,1)S(1)} %get-tuple-element.9.grad_in, ...), custom_call_target="tpu_custom_call" | custom-call | tf_op jit(solution)/shard_map/pallas_call | solution.py:539

commit v5 on v4

--- a/solution.py
+++ b/solution.py
@@ -69,7 +69,7 @@
 
     def piece(g, c):
         if g == 0:
-            return pl.ds(0, part) if c == 0 else pl.ds(part, rows - part)
+            return pl.ds(0, 2 * part) if c == 0 else pl.ds(2 * part, rows - 2 * part)
         return moving(c)
 
     def stash_load(c):
@@ -89,11 +89,12 @@
             ("angle", angle_hbm, angle_ref),
         ])
     }
-    stash_load(0).start()
     barrier = pltpu.get_barrier_semaphore()
     pl.semaphore_signal(barrier, inc=1, device_id={"fsdp": partner}, device_id_type=MESH)
     for j in range(1, chips):
         pl.semaphore_signal(barrier, inc=1, device_id={"fsdp": at_chip(j, core)}, device_id_type=MESH)
+
+    stash_load(0).start()
 
     @pl.when(not_last)
     def _():

time: 78.8 us -> 78.8 us (level)
  no operation moved by 1% of the time
where the time goes in v5:
time: 78.8 us; the launch traced here: 78.6 us
  Pallas kernels  77.4 us (98%)
  between operations  1.29 us (2%)
    pallas_call x1, Pallas kernels, local(): pl.pallas_call(functools.partial(kernel, sections, shards), out_shape=tup...  73.3 us
    pallas_call x1, Pallas kernels, local(): pl.pallas_call(functools.partial(store, 8), out_shape=tuple((jax.ShapeDty...  4.03 us

profile of v5, /device:TPU:0, one launch (start us, length us, event | category | flops | bytes accessed | tf_op | source)
XLA Modules:
  0.0 78.6 jit_solution(1838017641202198455)
XLA Ops:
  1.3 73.3 %shard_map.156 = (bf16[1,512,1024]{2,1,0:T(8,128)(2,1)S(1)}, bf16[1,512,1024]{2,1,0:T(8,128)(2,1)S(1)}, bf16[1,4096,1024]{2,1,0:T(8,128)(2,1)S(1)}, f32[1,1024]{1,0:T(1,128)S(1)}) custom-call(bf16[1,512,1024]{2,1,0:T(8,128)(2,1)} %act_hbm.1, bf16[1,512,1024]{2,1,0:T(8,128)(2,1)} %grad_hbm.1, bf16[1,2,512,1024]{3,2,1,0:T(8,128)(2,1)} %stash_hbm.1, ...), custom_call_target="tpu_custom_call" | custom-call | flops 12884901888 | bytes 20971520 | tf_op jit(solution)/shard_map/pallas_call | solution.py:486
  74.6 4.0 %shard_map.157 = (bf16[1,512,1024]{2,1,0:T(8,128)(2,1)}, bf16[1,512,1024]{2,1,0:T(8,128)(2,1)}, bf16[1,4096,1024]{2,1,0:T(8,128)(2,1)}, f32[1,1024]{1,0:T(1,128)}) custom-call(bf16[1,512,1024]{2,1,0:T(8,128)(2,1)S(1)} %get-tuple-element.8.fwd, bf16[1,512,1024]{2,1,0:T(8,128)(2,1)S(1)} %get-tuple-element.9.grad_in, ...), custom_call_target="tpu_custom_call" | custom-call | tf_op jit(solution)/shard_map/pallas_call | solution.py:540
